TPU v7x, 256 devices: a whole 4x4x8 slice. The times are simulated.
256 devices in a mesh: pipe: 8 (over y_hi, x), expert: 32 (over y_lo, z, core).
Axes of the slice: x: 4, y: 4 (y_hi: 2, y_lo: 2; y = y_hi * 2 + y_lo), z: 8, core: 2. Of those that a mesh axis runs over, the one named last changes fastest.
Arguments:
- fwd_in: bfloat16 [8, 4096, 3584], P('pipe', 'expert'), may hold values from -6 to 6
- fwd_route: int32 [8, 4096, 1], P('pipe', 'expert'), may hold values from 0 to 7; in each aligned block of 128 rows (0 to 127, 128 to 255, ..., all dimensions but the last counted through in order) at most 20 rows name the same one
- fwd_gate: float32 [8, 4096, 1], P('pipe', 'expert'), may hold values from 0.1 to 1
- bwd_saved: bfloat16 [8, 4096, 3584], P('pipe', 'expert'), may hold values from -6 to 6
- bwd_route: int32 [8, 4096, 1], P('pipe', 'expert'), may hold values from 0 to 7; in each aligned block of 128 rows (0 to 127, 128 to 255, ..., all dimensions but the last counted through in order) at most 20 rows name the same one
- bwd_gate: float32 [8, 4096, 1], P('pipe', 'expert'), may hold values from 0.1 to 1
- bwd_grad: bfloat16 [8, 4096, 3584], P('pipe', 'expert'), may hold values from -6 to 6
- w_in: bfloat16 [8, 32, 3584, 768], P('pipe', 'expert'), may hold values from -0.09375 to 0.09375
- w_out: bfloat16 [8, 32, 384, 3584], P('pipe', 'expert'), may hold values from -0.15625 to 0.15625
Outputs:
- fwd_out: bfloat16 [8, 4096, 3584], P('pipe', 'expert')
- bwd_out: bfloat16 [8, 4096, 3584], P('pipe', 'expert')
Inputs may be any that keep to these rules, and one draw needn't show every extreme that they name: `fwd_route`: within the 128 rows of one device, no expert id is named by more than 20 rows. `bwd_route`: within the 128 rows of one device, no expert id is named by more than 20 rows.
All inputs are finite; a program needn't handle non-finite values.
Results may differ from a plain program's by a relative error of at most 0.0035.
Values may be sent and summed in bfloat16 or wider, within the bound.
A program may use at most 128 MiB of HBM per device.

v0:
```python
import jax
import jax.numpy as jnp
from jax import lax
from jax.sharding import PartitionSpec as P

SPLIT = 4
TOP = 1


def shifted(block, axis, distance):
    devices = range(lax.axis_size(axis))
    route = [((i - distance) % len(devices), i) for i in devices]
    return lax.ppermute(block, axis, route)


def slice_forward(row_block, weight_in, weight_out):
    pre_act = jnp.dot(row_block, weight_in, preferred_element_type=jnp.float32)
    unit_count = weight_out.shape[0]
    gate_act = pre_act[:, :unit_count]
    up_act = pre_act[:, unit_count:]
    hidden = (gate_act * jax.nn.sigmoid(gate_act) * up_act).astype(jnp.bfloat16)
    return jnp.dot(hidden, weight_out, preferred_element_type=jnp.float32).astype(jnp.bfloat16)


def slice_backward(row_block, grad_block, weight_in, weight_out):
    pre_act = jnp.dot(row_block, weight_in, preferred_element_type=jnp.float32)
    unit_count = weight_out.shape[0]
    gate_act = pre_act[:, :unit_count]
    up_act = pre_act[:, unit_count:]
    sigmoid_gate = jax.nn.sigmoid(gate_act)
    hidden_grad = jnp.dot(grad_block, weight_out.T, preferred_element_type=jnp.float32)
    up_grad = hidden_grad * (gate_act * sigmoid_gate)
    gate_grad = hidden_grad * up_act * (sigmoid_gate * (1.0 + gate_act * (1.0 - sigmoid_gate)))
    pre_grad = jnp.concatenate([gate_grad, up_grad], axis=1).astype(jnp.bfloat16)
    return jnp.dot(pre_grad, weight_in.T, preferred_element_type=jnp.float32).astype(jnp.bfloat16)


def routing_tables(routing, gate_prob, experts, capacity):
    tok_count = routing.shape[0]
    top_count = routing.shape[1]
    onehot = (routing[:, :, None] == jnp.arange(experts, dtype=jnp.int32)[None, None, :]).astype(
        jnp.int32
    )
    flat_hits = onehot.reshape(tok_count * top_count, experts)
    earlier = jnp.cumsum(flat_hits, axis=0) - flat_hits
    slot_index = jnp.sum(earlier * flat_hits, axis=1).reshape(tok_count, top_count)
    target = routing * capacity + slot_index
    matches = target[:, :, None] == jnp.arange(experts * capacity, dtype=jnp.int32)[None, None, :]
    send_matrix = jnp.sum(matches.astype(jnp.float32), axis=1).T.astype(jnp.bfloat16)
    combine_matrix = jnp.sum(jnp.where(matches, gate_prob[:, :, None], 0.0), axis=1)
    return (send_matrix, combine_matrix)


def local(fwd_in, fwd_route, fwd_gate, bwd_saved, bwd_route, bwd_gate, bwd_grad, w_in, w_out):
    members = lax.axis_size("expert")
    experts = members // SPLIT
    tok_rows = fwd_in.shape[1]
    capacity = min(tok_rows, 5 * tok_rows * TOP // (4 * experts))
    weight_in = w_in[0, 0]
    weight_out = w_out[0, 0]
    arrived = shifted(fwd_in[0], "pipe", 1)
    returned = shifted(bwd_grad[0], "pipe", -1)
    saved = bwd_saved[0]
    fwd_send, fwd_combine = routing_tables(fwd_route[0], fwd_gate[0], experts, capacity)
    bwd_send, bwd_combine = routing_tables(bwd_route[0], bwd_gate[0], experts, capacity)

    def spread(send_matrix, values):
        buffer = jnp.dot(send_matrix, values, preferred_element_type=jnp.float32).astype(
            jnp.bfloat16
        )
        return jnp.repeat(buffer.reshape(experts, capacity, values.shape[1]), SPLIT, axis=0)

    def collect(partials, combine_matrix):
        width_all = partials.shape[2]
        summed = jnp.sum(
            partials.astype(jnp.float32).reshape(experts, SPLIT, capacity, width_all), axis=1
        )
        summed = summed.reshape(experts * capacity, width_all)
        return jnp.dot(
            combine_matrix,
            summed,
            precision=lax.Precision.HIGHEST,
            preferred_element_type=jnp.float32,
        )

    received = lax.all_to_all(
        spread(fwd_send, arrived), "expert", split_axis=0, concat_axis=0, tiled=True
    )
    count = received.shape[1]
    flat_rows = received.reshape(members * count, received.shape[2])
    fwd_parts = lax.all_to_all(
        slice_forward(flat_rows, weight_in, weight_out).reshape(members, count, received.shape[2]),
        "expert",
        split_axis=0,
        concat_axis=0,
        tiled=True,
    )
    received = (
        lax.all_to_all(spread(bwd_send, saved), "expert", split_axis=0, concat_axis=0, tiled=True),
        lax.all_to_all(
            spread(bwd_send, returned), "expert", split_axis=0, concat_axis=0, tiled=True
        ),
    )
    received_rows = received[0]
    received_grads = received[1]
    count = received_rows.shape[1]
    flat_rows = received_rows.reshape(members * count, received_rows.shape[2])
    flat_grads = received_grads.reshape(members * count, received_grads.shape[2])
    bwd_parts = lax.all_to_all(
        slice_backward(flat_rows, flat_grads, weight_in, weight_out).reshape(
            members, count, received_rows.shape[2]
        ),
        "expert",
        split_axis=0,
        concat_axis=0,
        tiled=True,
    )
    fwd_out = (arrived.astype(jnp.float32) + collect(fwd_parts, fwd_combine)).astype(jnp.bfloat16)
    bwd_out = (returned.astype(jnp.float32) + collect(bwd_parts, bwd_combine)).astype(jnp.bfloat16)
    return (fwd_out[None], bwd_out[None])


def solution(mesh):
    return jax.shard_map(
        local,
        mesh=mesh,
        in_specs=(
            P("pipe", "expert", None),
            P("pipe", "expert", None),
            P("pipe", "expert", None),
            P("pipe", "expert", None),
            P("pipe", "expert", None),
            P("pipe", "expert", None),
            P("pipe", "expert", None),
            P("pipe", "expert", None, None),
            P("pipe", "expert", None, None),
        ),
        out_specs=(P("pipe", "expert", None), P("pipe", "expert", None)),
        check_vma=False,
    )
```

profile of v0, /device:TPU:8, one launch (start us, length us, event | category | flops | bytes accessed | tf_op | source)
XLA Modules:
  0.0 703.5 jit_solution(1002733055610125662)
XLA Ops:
  0.6 0.0 copy-start
  0.6 0.9 fusion.29
  1.5 0.2 reduce_window_sum.18
  1.7 0.8 select_reduce_fusion
  2.5 0.7 multiply_add_fusion
  3.2 2.6 convolution_convert_fusion.2
  5.8 2.3 reshape.307
  8.1 4.2 broadcast_in_dim.51
  12.3 10.3 %all-to-all-start.3 = ((bf16[32,20,3584]{2,1,0:T(8,128)(2,1)}), bf16[32,20,3584]{2,1,0:T(8,128)(2,1)}, u32[]{:S(2)}, u32[]{:S(2)}) async-start(bf16[32,20,3584]{2,1,0:T(8,128)(2,1)} %bitcast.55), calls=%async_computation.3 | async-start | bytes 11010048 | tf_op jit(solution)/shard_map/all_to_all | solution.py:99
  22.6 1.6 collective-permute-start
  24.2 0.1 fusion.30
  24.2 0.2 reduce_window_sum.17
  24.4 0.2 select_reduce_fusion.1
  24.6 38.0 %collective-permute-done = bf16[128,3584]{1,0:T(8,128)(2,1)} collective-permute-done((bf16[128,3584]{1,0:T(8,128)(2,1)}, bf16[128,3584]{1,0:T(8,128)(2,1)}, u32[]{:S(2)}, u32[]{:S(2)}) %collective-permute-start) | collective-permute-done | bytes 917536 | tf_op jit(solution)/shard_map/ppermute | solution.py:13
  62.6 2.7 convolution_convert_fusion.4
  65.3 2.3 reshape.297
  67.6 82.2 %all-to-all-done.3 = bf16[32,20,3584]{2,1,0:T(8,128)(2,1)} async-done(((bf16[32,20,3584]{2,1,0:T(8,128)(2,1)}), bf16[32,20,3584]{2,1,0:T(8,128)(2,1)}, u32[]{:S(2)}, u32[]{:S(2)}) %all-to-all-start.3) | async-done | bytes 4587552 | tf_op jit(solution)/shard_map/all_to_all | solution.py:99
  149.8 4.1 broadcast_in_dim.46
  153.9 14.2 %all-to-all-start = ((bf16[32,20,3584]{2,1,0:T(8,128)(2,1)}), bf16[32,20,3584]{2,1,0:T(8,128)(2,1)}, u32[]{:S(2)}, u32[]{:S(2)}) async-start(bf16[32,20,3584]{2,1,0:T(8,128)(2,1)} %bitcast.56), calls=%async_computation | async-start | bytes 11010048 | tf_op jit(solution)/shard_map/all_to_all | solution.py:86
  168.1 0.1 collective-permute-start.1
  168.2 31.9 %collective-permute-done.1 = bf16[128,3584]{1,0:T(8,128)(2,1)S(1)} collective-permute-done((bf16[128,3584]{1,0:T(8,128)(2,1)}, bf16[128,3584]{1,0:T(8,128)(2,1)S(1)}, u32[]{:S(2)}, u32[]{:S(2)}) %collective-permute-start.1) | collective-permute-done | bytes 917536 | tf_op jit(solution)/shard_map/ppermute | solution.py:13
  200.1 0.9 copy-done.2
  201.0 1.5 convolution_convert_fusion.3
  202.5 2.3 reshape.304
  204.8 85.6 %all-to-all-done = bf16[32,20,3584]{2,1,0:T(8,128)(2,1)} async-done(((bf16[32,20,3584]{2,1,0:T(8,128)(2,1)}), bf16[32,20,3584]{2,1,0:T(8,128)(2,1)}, u32[]{:S(2)}, u32[]{:S(2)}) %all-to-all-start) | async-done | bytes 4587552 | tf_op jit(solution)/shard_map/all_to_all | solution.py:86
  290.5 4.2 broadcast_in_dim.50
  294.7 8.6 %all-to-all-start.2 = ((bf16[32,20,3584]{2,1,0:T(8,128)(2,1)}), bf16[32,20,3584]{2,1,0:T(8,128)(2,1)}, u32[]{:S(2)}, u32[]{:S(2)}) async-start(bf16[32,20,3584]{2,1,0:T(8,128)(2,1)} %bitcast.57), calls=%async_computation.2 | async-start | bytes 11010048 | tf_op jit(solution)/shard_map/all_to_all | solution.py:100
  303.3 7.3 %reshape.299 = bf16[640,3584]{1,0:T(8,128)(2,1)} reshape(bf16[32,20,3584]{2,1,0:T(8,128)(2,1)} %all-to-all-done) | data formatting | bytes 9175040 | tf_op jit(solution)/shard_map/reshape | solution.py:90
  310.6 7.2 %fusion.3 = f32[640,768]{1,0:T(8,128)S(1)} fusion(bf16[640,3584]{1,0:T(8,128)(2,1)} %reshape.299, bf16[1,1,3584,768]{3,2,1,0:T(8,128)(2,1)} %param.16), kind=kOutput, calls=%fused_computation.7 | convolution fusion | flops 3523215360 | bytes 12058624 | tf_op jit(solution)/shard_map/dot_general | solution.py:17
  317.8 4.8 convolution_convert_fusion.1
  322.5 7.2 %reshape.300 = bf16[32,20,3584]{2,1,0:T(8,128)(2,1)} reshape(bf16[640,3584]{1,0:T(8,128)(2,1)} %convolution_convert_fusion.1) | data formatting | bytes 9175040 | tf_op jit(solution)/shard_map/reshape | solution.py:92
  329.7 95.9 %all-to-all-done.2 = bf16[32,20,3584]{2,1,0:T(8,128)(2,1)} async-done(((bf16[32,20,3584]{2,1,0:T(8,128)(2,1)}), bf16[32,20,3584]{2,1,0:T(8,128)(2,1)}, u32[]{:S(2)}, u32[]{:S(2)}) %all-to-all-start.2) | async-done | bytes 4587552 | tf_op jit(solution)/shard_map/all_to_all | solution.py:100
  425.6 8.6 %all-to-all-start.1 = ((bf16[32,20,3584]{2,1,0:T(8,128)(2,1)}), bf16[32,20,3584]{2,1,0:T(8,128)(2,1)}, u32[]{:S(2)}, u32[]{:S(2)}) async-start(bf16[32,20,3584]{2,1,0:T(8,128)(2,1)} %reshape.300), calls=%async_computation.1 | async-start | bytes 11010048 | tf_op jit(solution)/shard_map/all_to_all | solution.py:91
  434.2 7.3 %reshape.309 = bf16[640,3584]{1,0:T(8,128)(2,1)} reshape(bf16[32,20,3584]{2,1,0:T(8,128)(2,1)} %all-to-all-done.3) | data formatting | bytes 9175040 | tf_op jit(solution)/shard_map/reshape | solution.py:107
  441.6 9.0 %fusion.1 = f32[640,768]{1,0:T(8,128)} fusion(bf16[640,3584]{1,0:T(8,128)(2,1)} %reshape.309, bf16[1,1,3584,768]{3,2,1,0:T(8,128)(2,1)} %param.16), kind=kOutput, calls=%fused_computation.5 | convolution fusion | flops 3523215360 | bytes 12058624 | tf_op jit(solution)/shard_map/dot_general | solution.py:26
  450.5 7.3 %reshape.306 = bf16[640,3584]{1,0:T(8,128)(2,1)} reshape(bf16[32,20,3584]{2,1,0:T(8,128)(2,1)} %all-to-all-done.2) | data formatting | bytes 9175040 | tf_op jit(solution)/shard_map/reshape | solution.py:108
  457.9 5.6 fusion.9
  463.5 8.0 %convolution_convert_fusion = bf16[640,3584]{1,0:T(8,128)(2,1)} fusion(bf16[1,1,3584,768]{3,2,1,0:T(8,128)(2,1)} %param.16, bf16[640,384]{1,0:T(8,128)(2,1)S(1)} %get-tuple-element.3, bf16[640,384]{1,0:T(8,128)(2,1)S(1)} %get-tuple-element.2), kind=kOutput, calls=%fused_computation.2 | convolution fusion | flops 3527475200 | bytes 11075584 | tf_op jit(solution)/shard_map/dot_general | solution.py:35
  471.5 7.2 %reshape.310 = bf16[32,20,3584]{2,1,0:T(8,128)(2,1)} reshape(bf16[640,3584]{1,0:T(8,128)(2,1)} %convolution_convert_fusion) | data formatting | bytes 9175040 | tf_op jit(solution)/shard_map/reshape | solution.py:110
  478.7 77.9 %all-to-all-done.1 = bf16[32,20,3584]{2,1,0:T(8,128)(2,1)} async-done(((bf16[32,20,3584]{2,1,0:T(8,128)(2,1)}), bf16[32,20,3584]{2,1,0:T(8,128)(2,1)}, u32[]{:S(2)}, u32[]{:S(2)}) %all-to-all-start.1) | async-done | bytes 4587552 | tf_op jit(solution)/shard_map/all_to_all | solution.py:91
  556.6 8.6 %all-to-all-start.4 = ((bf16[32,20,3584]{2,1,0:T(8,128)(2,1)}), bf16[32,20,3584]{2,1,0:T(8,128)(2,1)}, u32[]{:S(2)}, u32[]{:S(2)}) async-start(bf16[32,20,3584]{2,1,0:T(8,128)(2,1)} %reshape.310), calls=%async_computation.4 | async-start | bytes 11010048 | tf_op jit(solution)/shard_map/all_to_all | solution.py:109
  565.2 5.3 convert_reduce_fusion.1
  570.5 3.0 reshape.303
  573.4 114.2 %all-to-all-done.4 = bf16[32,20,3584]{2,1,0:T(8,128)(2,1)} async-done(((bf16[32,20,3584]{2,1,0:T(8,128)(2,1)}), bf16[32,20,3584]{2,1,0:T(8,128)(2,1)}, u32[]{:S(2)}, u32[]{:S(2)}) %all-to-all-start.4) | async-done | bytes 4587552 | tf_op jit(solution)/shard_map/all_to_all | solution.py:109
  687.6 5.3 convert_reduce_fusion
  692.9 2.9 reshape.313
  695.8 4.8 fusion.14
  700.6 2.9 fusion.15
  (13 shorter events, 0.0 us)
Async XLA Ops:
  0.6 317.1 %copy-start = (bf16[1,1,384,3584]{3,2,1,0:T(8,128)(2,1)S(1)}, bf16[1,1,384,3584]{3,2,1,0:T(8,128)(2,1)}, u32[]{:S(2)}) copy-start(bf16[1,1,384,3584]{3,2,1,0:T(8,128)(2,1)} %param.17) | copy-start | bytes 8257540
  12.3 11.9 %copy-start.4 = (s32[1,128,1]{1,2,0:T(1,128)S(1)}, s32[1,128,1]{1,2,0:T(1,128)}, u32[]{:S(2)}) copy-start(s32[1,128,1]{1,2,0:T(1,128)} %param.10) | copy-start | bytes 1540
  12.3 137.5 %all-to-all-start.3 = ((bf16[32,20,3584]{2,1,0:T(8,128)(2,1)}), bf16[32,20,3584]{2,1,0:T(8,128)(2,1)}, u32[]{:S(2)}, u32[]{:S(2)}) async-start(bf16[32,20,3584]{2,1,0:T(8,128)(2,1)} %bitcast.55), calls=%async_computation.3 | async-start | bytes 11010048 | tf_op jit(solution)/shard_map/all_to_all | solution.py:99
  22.6 40.0 %collective-permute-start = (bf16[128,3584]{1,0:T(8,128)(2,1)}, bf16[128,3584]{1,0:T(8,128)(2,1)}, u32[]{:S(2)}, u32[]{:S(2)}) collective-permute-start(bf16[128,3584]{1,0:T(8,128)(2,1)} %bitcast.64), channel_id=1, source_target_pairs={{224,0},{0,32},{32,64},{64,96},{96,128},{128,160},{160,192},{192,2... | collective-permute-start | bytes 2752520 | tf_op jit(solution)/shard_map/ppermute | solution.py:13
  153.9 136.5 %all-to-all-start = ((bf16[32,20,3584]{2,1,0:T(8,128)(2,1)}), bf16[32,20,3584]{2,1,0:T(8,128)(2,1)}, u32[]{:S(2)}, u32[]{:S(2)}) async-start(bf16[32,20,3584]{2,1,0:T(8,128)(2,1)} %bitcast.56), calls=%async_computation | async-start | bytes 11010048 | tf_op jit(solution)/shard_map/all_to_all | solution.py:86
  168.1 32.0 %collective-permute-start.1 = (bf16[128,3584]{1,0:T(8,128)(2,1)}, bf16[128,3584]{1,0:T(8,128)(2,1)S(1)}, u32[]{:S(2)}, u32[]{:S(2)}) collective-permute-start(bf16[128,3584]{1,0:T(8,128)(2,1)} %bitcast.65), channel_id=1, source_target_pairs={{32,0},{64,32},{96,64},{128,96},{160,128},{192,160},{224,192},{0,2... | collective-permute-start | bytes 2752520 | tf_op jit(solution)/shard_map/ppermute | solution.py:13
  200.1 0.9 copy-start.2
  294.7 131.0 %all-to-all-start.2 = ((bf16[32,20,3584]{2,1,0:T(8,128)(2,1)}), bf16[32,20,3584]{2,1,0:T(8,128)(2,1)}, u32[]{:S(2)}, u32[]{:S(2)}) async-start(bf16[32,20,3584]{2,1,0:T(8,128)(2,1)} %bitcast.57), calls=%async_computation.2 | async-start | bytes 11010048 | tf_op jit(solution)/shard_map/all_to_all | solution.py:100
  425.6 131.0 %all-to-all-start.1 = ((bf16[32,20,3584]{2,1,0:T(8,128)(2,1)}), bf16[32,20,3584]{2,1,0:T(8,128)(2,1)}, u32[]{:S(2)}, u32[]{:S(2)}) async-start(bf16[32,20,3584]{2,1,0:T(8,128)(2,1)} %reshape.300), calls=%async_computation.1 | async-start | bytes 11010048 | tf_op jit(solution)/shard_map/all_to_all | solution.py:91
  556.6 131.0 %all-to-all-start.4 = ((bf16[32,20,3584]{2,1,0:T(8,128)(2,1)}), bf16[32,20,3584]{2,1,0:T(8,128)(2,1)}, u32[]{:S(2)}, u32[]{:S(2)}) async-start(bf16[32,20,3584]{2,1,0:T(8,128)(2,1)} %reshape.310), calls=%async_computation.4 | async-start | bytes 11010048 | tf_op jit(solution)/shard_map/all_to_all | solution.py:109
  692.9 2.9 copy-start.5
  695.8 4.8 copy-start.1
  695.8 4.8 copy-start.3
  695.8 4.8 copy-start.6
where the time goes:
time: 708 us; the launch traced here: 704 us
  waiting for transfers between devices  526 us (74%)
  local copies, waits for them, and re-layouts  62.6 us (9%)
  starting transfers between devices  51.9 us (7%)
  matrix products  49 us (7%)
  other arithmetic  13.5 us (2%)
    all_to_all x1, waiting for transfers between devices, local(): lax.all_to_all(slice_backward(flat_rows, flat_grads, weight_in, weight_ou...  114 us
    all_to_all x1, waiting for transfers between devices, local(): lax.all_to_all(spread(bwd_send, returned), 'expert', split_axis=0, concat...  95.9 us
    all_to_all x1, waiting for transfers between devices, local(): lax.all_to_all(spread(fwd_send, arrived), 'expert', split_axis=0, concat_...  85.6 us
    all_to_all x1, waiting for transfers between devices, local(): lax.all_to_all(spread(bwd_send, saved), 'expert', split_axis=0, concat_ax...  82.2 us
    all_to_all x1, waiting for transfers between devices, local(): lax.all_to_all(slice_forward(flat_rows, weight_in, weight_out).reshape(me...  77.9 us
    ppermute x2, waiting for transfers between devices, shifted(): return lax.ppermute(block, axis, route)  69.9 us
    all_to_all x1, starting transfers between devices, local(): lax.all_to_all(spread(fwd_send, arrived), 'expert', split_axis=0, concat_...  14.2 us
  transfers between devices with their start and end apart: 7, of which 7 were waited for; matrix products, arithmetic and copies ran while one was open for 13% of the time, Pallas kernels for 0%

commit v1 on v0

v1 whole, which is shorter than its diff:
```python
import jax
import jax.numpy as jnp
from jax import lax
from jax.experimental import pallas as pl
from jax.experimental.pallas import tpu as pltpu
from jax.sharding import PartitionSpec as P

MESH = pl.DeviceIdType.MESH
TOK = 128
D = 3584
HID = 384
ROWS = 16
CHUNK = 896
CHUNKS = 4
FOLD = 4
UNITS = 8
ENTRY = UNITS * ROWS
ALL_ROWS = 4 * ENTRY
LEFT = 128
OFFSETS = (0, -1, 2, -3)
ORDER = (4, 0, 1, 2, 3)
SAVED, ARRIVED, RETURNED = 0, 1, 2
FORWARD, BACKWARD = 0, 1
F32 = jnp.float32
BF16 = jnp.bfloat16


def dot(a, b):
    return lax.dot_general(a, b, (((1,), (0,)), ((), ())), preferred_element_type=F32)


def dot_t(a, b):
    return lax.dot_general(a, b, (((1,), (1,)), ((), ())), preferred_element_type=F32)


def iota(shape, dim):
    return lax.broadcasted_iota(jnp.int32, shape, dim)


def one_hot(mask):
    return jnp.where(mask, 1.0, 0.0).astype(BF16)


def kernel(
    fwd_in, fwd_route, fwd_gate, bwd_saved, bwd_route, bwd_gate, bwd_grad, w_in, w_out,
    fwd_out, bwd_out,
    saved, arrived, returned, win, wout, packed, land, pre_f, pre_b, hidden, pre_grad,
    own, cross, sib, pair_out, pair_in, total, back, result,
    send_a, recv_a, send_b, recv_b, send_c, recv_c, send_d, recv_d,
    send_s, recv_s, send_p, recv_p, send_r, recv_r, send_m, recv_m, load, store,
):
    pipe = lax.axis_index("pipe")
    place = lax.axis_index("expert")
    y = lax.div(place, 16)
    z = lax.rem(lax.div(place, 2), 8)
    core = lax.rem(place, 2)
    side = 1 - 2 * lax.rem(z, 2)

    def device(pipe_at, y_at, z_at, core_at):
        return (pipe_at, y_at * 16 + z_at * 2 + core_at)

    def at(y_step, z_step):
        return lax.rem(y + y_step, 2), lax.rem(z + z_step + 8, 8)

    targets, experts, sources = [], [], []
    for i in range(4):
        for y_step in range(2):
            y_to, z_to = at(y_step, OFFSETS[i] * side)
            targets.append(device(pipe, y_to, z_to, core))
            experts.append(y_to * 4 + lax.div(z_to, 2))
            y_from, z_from = at(y_step, -i * side)
            sources.append(device(pipe, y_from, z_from, core))
    sibling = device(pipe, y, z, 1 - core)
    partner = device(pipe, y, lax.rem(z + side + 8, 8), core)
    after = (lax.rem(pipe + 1, 8), place)
    before = (lax.rem(pipe + 7, 8), place)

    loads = [pltpu.make_async_copy(bwd_saved, saved, load.at[0])]
    for k in range(CHUNKS):
        columns = pl.ds(k * CHUNK, CHUNK)
        loads.append(pltpu.make_async_copy(w_in.at[columns], win.at[k], load.at[1 + k]))
        loads.append(pltpu.make_async_copy(w_out.at[:, columns], wout.at[k], load.at[5 + k]))
    for copy in loads:
        copy.start()

    barrier = pltpu.get_barrier_semaphore()
    peers = targets[1:] + sources[4:6] + [sibling, partner, after, before]
    for peer in peers:
        pl.semaphore_signal(barrier, inc=1, device_id=peer, device_id_type=MESH)
    pl.semaphore_wait(barrier, len(peers))

    def remote(src, dst, send, recv, to):
        return pltpu.make_async_remote_copy(
            src_ref=src, dst_ref=dst, send_sem=send, recv_sem=recv, device_id=to, device_id_type=MESH
        )

    moves = [
        remote(fwd_in, arrived, send_m.at[0], recv_m.at[0], after),
        remote(bwd_grad, returned, send_m.at[1], recv_m.at[1], before),
    ]
    for copy in moves:
        copy.start()

    def unit_experts(shape, dim):
        unit = lax.div(iota(shape, dim), ROWS)
        named = jnp.zeros(shape, jnp.int32)
        for u in range(UNITS):
            named = jnp.where(unit == u, experts[u], named)
        return named

    def pack(flow, values, route):
        square = (TOK, TOK)
        by_row = jnp.broadcast_to(route[...], square).astype(F32)
        by_lane = by_row.T
        earlier = iota(square, 0) < iota(square, 1)
        slot = jnp.sum(jnp.where((by_row == by_lane) & earlier, 1.0, 0.0), axis=0, keepdims=True)
        named = unit_experts(square, 0).astype(F32) == by_lane
        row = lax.rem(iota(square, 0), ROWS)
        main = one_hot(named & (row.astype(F32) == slot))
        late = named & ((ROWS + lax.rem(row, 4)).astype(F32) == slot)

        def put(k, rows):
            packed[flow, k] = rows.astype(BF16)
            land[flow, k, 0:ROWS] = packed[flow, k, 0:ROWS]
            for u in range(1, UNITS):
                block = pl.ds(u * ROWS, ROWS)
                remote(
                    packed.at[flow, k, block], land.at[flow, k, block],
                    send_a.at[flow, k], recv_a.at[flow, k], targets[u],
                ).start()

        for k in range(CHUNKS):
            put(k, dot(main, values[:, k * CHUNK : (k + 1) * CHUNK]))
        rows = jnp.zeros((ENTRY, CHUNK), F32)
        for k in range(CHUNKS):
            mine = one_hot(late & (lax.div(row, 4) == k))
            rows = rows + dot(mine, values[:, k * CHUNK : (k + 1) * CHUNK])
        put(FOLD, rows)

    def direct(flow, k):
        block = pl.ds(ROWS, ENTRY - ROWS)
        return remote(
            packed.at[flow, k, block], land.at[flow, k, block],
            send_a.at[flow, k], recv_a.at[flow, k], targets[1],
        )

    def group(flow, k, index):
        return land.at[flow, k, pl.ds(index * ENTRY, ENTRY)]

    def to_partner(flow, k):
        return remote(
            group(flow, k, 0), group(flow, k, 1), send_b.at[flow, k], recv_b.at[flow, k], partner
        )

    def to_sibling(flow, k):
        return remote(
            group(flow, k, 0), group(flow, k, 2), send_c.at[flow, k], recv_c.at[flow, k], sibling
        )

    def on_to_sibling(flow, k):
        return remote(
            group(flow, k, 1), group(flow, k, 3), send_d.at[flow, k], recv_d.at[flow, k], sibling
        )

    def enter(flow, k):
        direct(flow, k).wait_recv()
        to_partner(flow, k).start()
        to_sibling(flow, k).start()

    def pass_on(flow, k):
        to_partner(flow, k).wait_recv()
        on_to_sibling(flow, k).start()

    def ready(flow):
        for k in range(CHUNKS + 1):
            to_sibling(flow, k).wait_recv()
            on_to_sibling(flow, k).wait_recv()

    def unfold(flow, k):
        shape = (LEFT, ALL_ROWS)
        row = iota(shape, 0)
        taken = lax.div(row, 4) * ROWS + k * 4 + lax.rem(row, 4)
        return dot(one_hot(iota(shape, 1) == taken), land[flow, FOLD]).astype(BF16)

    def fold(k, rows):
        shape = (ALL_ROWS, LEFT)
        column = iota(shape, 1)
        taken = lax.div(column, 4) * ROWS + k * 4 + lax.rem(column, 4)
        return dot(one_hot(iota(shape, 0) == taken), rows)

    def activate_in(flow, out):
        out[...] = jnp.zeros_like(out)

        @pl.loop(0, CHUNKS)
        def _(k):
            weight = win[k]
            out[0:ALL_ROWS] += dot(land[flow, k], weight)
            out[ALL_ROWS:] += dot(unfold(flow, k), weight)

    def make_hidden():
        @pl.loop(0, (ALL_ROWS + LEFT) // LEFT)
        def _(n):
            rows = pl.ds(pl.multiple_of(n * LEFT, LEFT), LEFT)
            gate_act = pre_f[rows, :HID]
            hidden[rows] = (gate_act * jax.nn.sigmoid(gate_act) * pre_f[rows, HID:]).astype(BF16)

    def make_pre_grad():
        pre_f[...] = jnp.zeros_like(pre_f)

        @pl.loop(0, CHUNKS)
        def _(k):
            weight = wout[k]
            pre_f[0:ALL_ROWS, :HID] += dot_t(land[RETURNED, k], weight)
            pre_f[ALL_ROWS:, :HID] += dot_t(unfold(RETURNED, k), weight)

        @pl.loop(0, (ALL_ROWS + LEFT) // LEFT)
        def _(n):
            rows = pl.ds(pl.multiple_of(n * LEFT, LEFT), LEFT)
            hidden_grad = pre_f[rows, :HID]
            gate_act = pre_b[rows, :HID]
            up_act = pre_b[rows, HID:]
            sigmoid_gate = jax.nn.sigmoid(gate_act)
            up_grad = hidden_grad * (gate_act * sigmoid_gate)
            slope = sigmoid_gate * (1.0 + gate_act * (1.0 - sigmoid_gate))
            pre_grad[rows, :HID] = (hidden_grad * up_act * slope).astype(BF16)
            pre_grad[rows, HID:] = up_grad.astype(BF16)

    def product(way, rows, k):
        if way == FORWARD:
            return dot(hidden[rows], wout[k])
        return dot_t(pre_grad[rows], win[k])

    def swap(way, k):
        return remote(cross.at[k], sib.at[way, k], send_s.at[way, k], recv_s.at[way, k], sibling)

    def to_exit(way, k):
        return remote(pair_out.at[k], pair_in.at[way, k], send_p.at[way, k], recv_p.at[way, k], partner)

    def homeward(way, k):
        block = pl.ds(ROWS, ENTRY - ROWS)
        return remote(
            total.at[k, block], back.at[way, k, block], send_r.at[way, k], recv_r.at[way, k], sources[1]
        )

    def work(way, k):
        if way == BACKWARD:
            swap(FORWARD, k).wait_send()
        if k < CHUNKS:
            rows = product(way, slice(0, ALL_ROWS), k).astype(BF16)
            own[k] = rows[: 2 * ENTRY]
            cross[k] = rows[2 * ENTRY :]
        else:
            rows = jnp.zeros((ALL_ROWS, CHUNK), F32)
            for c in range(CHUNKS):
                rows = rows + fold(c, product(way, slice(ALL_ROWS, ALL_ROWS + LEFT), c).astype(BF16))
            rows = rows.astype(BF16)
            own[k] = rows[: 2 * ENTRY]
            cross[k] = rows[2 * ENTRY :]
        swap(way, k).start()

    def add_sibling(way, k):
        swap(way, k).wait_recv()
        if way == BACKWARD:
            to_exit(FORWARD, k).wait_send()
        rows = own[k, ENTRY:].astype(F32) + sib[way, k, ENTRY:].astype(F32)
        pair_out[k] = rows.astype(BF16)
        to_exit(way, k).start()

    def leave(way, k):
        to_exit(way, k).wait_recv()
        if way == BACKWARD:
            homeward(FORWARD, k).wait_send()
        rows = own[k, :ENTRY].astype(F32) + sib[way, k, :ENTRY].astype(F32)
        total[k] = (rows + pair_in[way, k].astype(F32)).astype(BF16)
        back[way, k, 0:ROWS] = total[k, 0:ROWS]
        for u in range(1, UNITS):
            block = pl.ds(u * ROWS, ROWS)
            remote(
                total.at[k, block], back.at[way, k, block],
                send_r.at[way, k], recv_r.at[way, k], sources[u],
            ).start()

    def written(way, k):
        columns = pl.ds(k * CHUNK, CHUNK)
        out = fwd_out if way == FORWARD else bwd_out
        return pltpu.make_async_copy(result.at[way, :, columns], out.at[:, columns], store.at[way, k])

    def finish(way, k):
        homeward(way, k).wait_recv()
        if k == FOLD:
            return
        route, gate, base = (
            (fwd_route, fwd_gate, arrived) if way == FORWARD else (bwd_route, bwd_gate, returned)
        )
        square = (TOK, TOK)
        by_row = jnp.broadcast_to(route[...], square).astype(F32)
        by_lane = by_row.T
        earlier = iota(square, 1) < iota(square, 0)
        slot = jnp.sum(jnp.where((by_row == by_lane) & earlier, 1.0, 0.0), axis=1, keepdims=True)
        named = unit_experts(square, 1).astype(F32) == by_row
        column = lax.rem(iota(square, 1), ROWS)
        main = one_hot(named & (column.astype(F32) == slot))
        late = named & ((ROWS + lax.rem(column, 4)).astype(F32) == slot)
        mine = one_hot(late & (lax.div(column, 4) == k))
        mixture = dot(main, back[way, k]) + dot(mine, back[way, FOLD])
        at_columns = slice(k * CHUNK, (k + 1) * CHUNK)
        result[way, :, at_columns] = (
            base[:, at_columns].astype(F32) + gate[...] * mixture
        ).astype(BF16)
        written(way, k).start()

    loads[0].wait()
    pack(SAVED, saved, bwd_route)
    for k in range(CHUNKS + 1):
        enter(SAVED, k)
        if k:
            pass_on(SAVED, k - 1)
        if k == 3:
            moves[0].wait_recv()
            pack(ARRIVED, arrived, fwd_route)
    pass_on(SAVED, FOLD)
    for k in range(CHUNKS + 1):
        enter(ARRIVED, k)
        if k:
            pass_on(ARRIVED, k - 1)
        else:
            for copy in loads[1:]:
                copy.wait()
            ready(SAVED)
            activate_in(SAVED, pre_b)
        if k == 3:
            moves[1].wait_recv()
            pack(RETURNED, returned, bwd_route)
    pass_on(ARRIVED, FOLD)
    for k in range(CHUNKS + 1):
        enter(RETURNED, k)
        if k:
            pass_on(RETURNED, k - 1)
        else:
            ready(ARRIVED)
            activate_in(ARRIVED, pre_f)
            make_hidden()
        work(FORWARD, ORDER[k])
    pass_on(RETURNED, FOLD)
    for k in ORDER:
        add_sibling(FORWARD, k)
    ready(RETURNED)
    make_pre_grad()
    for j, k in enumerate(ORDER):
        leave(FORWARD, k)
        work(BACKWARD, k)
        if j:
            add_sibling(BACKWARD, ORDER[j - 1])
    add_sibling(BACKWARD, ORDER[-1])
    for k in ORDER:
        leave(BACKWARD, k)
        finish(FORWARD, k)
    for k in ORDER:
        finish(BACKWARD, k)

    for copy in moves:
        copy.wait_send()
    for flow in range(3):
        for k in range(CHUNKS + 1):
            direct(flow, k).wait_send()
            to_partner(flow, k).wait_send()
            to_sibling(flow, k).wait_send()
            on_to_sibling(flow, k).wait_send()
    for k in range(CHUNKS + 1):
        swap(BACKWARD, k).wait_send()
        to_exit(BACKWARD, k).wait_send()
        homeward(BACKWARD, k).wait_send()
    for way in (FORWARD, BACKWARD):
        for k in range(CHUNKS):
            written(way, k).wait()


def local(fwd_in, fwd_route, fwd_gate, bwd_saved, bwd_route, bwd_gate, bwd_grad, w_in, w_out):
    any_place = pl.BlockSpec(memory_space=pl.ANY)
    vmem = pl.BlockSpec(memory_space=pltpu.VMEM)
    tokens = (TOK, D)
    parts = CHUNKS + 1
    dma = pltpu.SemaphoreType.DMA
    fwd_out, bwd_out = pl.pallas_call(
        kernel,
        out_shape=[jax.ShapeDtypeStruct(tokens, BF16)] * 2,
        in_specs=[any_place, vmem, vmem, any_place, vmem, vmem, any_place, any_place, any_place],
        out_specs=[any_place, any_place],
        scratch_shapes=[
            pltpu.VMEM(tokens, BF16),
            pltpu.VMEM(tokens, BF16),
            pltpu.VMEM(tokens, BF16),
            pltpu.VMEM((CHUNKS, CHUNK, 2 * HID), BF16),
            pltpu.VMEM((CHUNKS, HID, CHUNK), BF16),
            pltpu.VMEM((3, parts, ENTRY, CHUNK), BF16),
            pltpu.VMEM((3, parts, ALL_ROWS, CHUNK), BF16),
            pltpu.VMEM((ALL_ROWS + LEFT, 2 * HID), F32),
            pltpu.VMEM((ALL_ROWS + LEFT, 2 * HID), F32),
            pltpu.VMEM((ALL_ROWS + LEFT, HID), BF16),
            pltpu.VMEM((ALL_ROWS + LEFT, 2 * HID), BF16),
            pltpu.VMEM((parts, 2 * ENTRY, CHUNK), BF16),
            pltpu.VMEM((parts, 2 * ENTRY, CHUNK), BF16),
            pltpu.VMEM((2, parts, 2 * ENTRY, CHUNK), BF16),
            pltpu.VMEM((parts, ENTRY, CHUNK), BF16),
            pltpu.VMEM((2, parts, ENTRY, CHUNK), BF16),
            pltpu.VMEM((parts, ENTRY, CHUNK), BF16),
            pltpu.VMEM((2, parts, ENTRY, CHUNK), BF16),
            pltpu.VMEM((2, TOK, D), BF16),
        ]
        + [dma((3, parts))] * 8
        + [dma((2, parts))] * 6
        + [dma((2,))] * 2
        + [dma((9,)), dma((2, CHUNKS))],
        compiler_params=pltpu.CompilerParams(
            collective_id=0, has_side_effects=True, vmem_limit_bytes=60 * 2**20
        ),
        cost_estimate=pl.CostEstimate(
            flops=14 * 10**9, bytes_accessed=14 * 10**6, transcendentals=500_000
        ),
    )(
        fwd_in[0], fwd_route[0], fwd_gate[0], bwd_saved[0], bwd_route[0], bwd_gate[0], bwd_grad[0],
        w_in[0, 0], w_out[0, 0],
    )
    return fwd_out[None], bwd_out[None]


def solution(mesh):
    rows = P("pipe", "expert", None)
    pieces = P("pipe", "expert", None, None)
    return jax.shard_map(
        local,
        mesh=mesh,
        in_specs=(rows,) * 7 + (pieces,) * 2,
        out_specs=(rows, rows),
        check_vma=False,
    )
```

time: 708 us -> 242 us (0.34)
  waiting for transfers between devices: 526 us -> 0 us
  Pallas kernels: 0 us -> 231 us
  local copies, waits for them, and re-layouts: 62.6 us -> 9.87 us
  starting transfers between devices: 51.9 us -> 0 us
  matrix products: 49 us -> 0 us
  other arithmetic: 13.5 us -> 0 us
    all_to_all x5 -> x0, waiting for transfers between devices: 456 us -> none  [the longest x1 114 us: local(): lax.all_to_all(slice_backward(flat_rows, flat_grads, weight_in, weight_ou...]
    pallas_call x0 -> x1, Pallas kernels: none -> 231 us  [local(): pl.pallas_call(kernel, out_shape=[jax.ShapeDtypeStruct(tokens, BF16)] * 2...]
    ppermute x2 -> x0, waiting for transfers between devices: 69.9 us -> none  [shifted(): return lax.ppermute(block, axis, route)]
    all_to_all x5 -> x0, starting transfers between devices: 50.2 us -> none  [the longest x1 14.2 us: local(): lax.all_to_all(spread(fwd_send, arrived), 'expert', split_axis=0, concat_...]
    reshape x10 -> x0, local copies, waits for them, and re-layouts: 49.1 us -> none  [the longest x1 7.33 us: local(): flat_rows = received_rows.reshape(members * count, received_rows.shape[2])]
    dot_general x10 -> x0, matrix products: 49 us -> none  [the longest x1 8.98 us: slice_backward(): pre_act = jnp.dot(row_block, weight_in, preferred_element_type=jnp.float32)]
    broadcast_in_dim x3 -> x0, local copies, waits for them, and re-layouts: 12.5 us -> none  [spread(): jnp.repeat(buffer.reshape(experts, capacity, values.shape[1]), SPLIT, axi...]
    reduce_sum x4 -> x0, other arithmetic: 11.6 us -> none  [the longest x2 10.6 us: collect(): jnp.sum(partials.astype(jnp.float32).reshape(experts, SPLIT, capacity, wi...]
  transfers between devices with their start and end apart: 7 -> 0, of which waited for: 7 -> 0; matrix products, arithmetic and copies ran while one was open for 13% -> 0% of each run, Pallas kernels for 0% -> 0%
where the time goes in v1:
time: 242 us
  Pallas kernels  231 us (95%)
  local copies, waits for them, and re-layouts  9.87 us (4%)
    pallas_call x1, Pallas kernels, local(): pl.pallas_call(kernel, out_shape=[jax.ShapeDtypeStruct(tokens, BF16)] * 2...  231 us

profile of v1, /device:TPU:8, one launch (start us, length us, event | category | flops | bytes accessed | tf_op | source)
XLA Modules:
  0.0 241.6 jit_solution(9237884910861826171)
XLA Ops:
  0.6 1.4 copy.11.fwd_route
  2.0 1.4 copy.12.fwd_gate
  3.4 1.4 copy.13.bwd_route
  4.8 1.4 copy.14.bwd_gate
  6.2 231.0 %shard_map.104 = (bf16[128,3584]{1,0:T(8,128)(2,1)}, bf16[128,3584]{1,0:T(8,128)(2,1)}) custom-call(bf16[128,3584]{1,0:T(8,128)(2,1)} %bitcast.19, s32[128,1]{1,0:T(8,128)} %copy.11.fwd_route, f32[128,1]{1,0:T(8,128)} %copy.12.fwd_gate, bf16[128,3584]{1,0:T(8,128)(2,1)} %bitcast.20, s32[128,1]{1,0:T(8,128)} %copy.13.bwd_route, f32[128,1]{1,0:T(8,128)} %copy.14.bwd_gate, ...), custom_call_target="tpu_custom_call" | custom-call | flops 14000000000 | bytes 14000000 | tf_op jit(solution)/shard_map/pallas_call | solution.py:384
  237.2 2.2 copy.17
  239.4 2.2 copy.18

commit v2 on v1

--- a/solution.py
+++ b/solution.py
@@ -18,7 +18,10 @@
 ALL_ROWS = 4 * ENTRY
 LEFT = 128
 OFFSETS = (0, -1, 2, -3)
-ORDER = (4, 0, 1, 2, 3)
+ORDER = (0, 4, 1, 2, 3)
+MOVE_AT = (0, 4)
+LAG = 4
+AHEAD = 5
 SAVED, ARRIVED, RETURNED = 0, 1, 2
 FORWARD, BACKWARD = 0, 1
 F32 = jnp.float32
@@ -44,7 +47,7 @@
 def kernel(
     fwd_in, fwd_route, fwd_gate, bwd_saved, bwd_route, bwd_gate, bwd_grad, w_in, w_out,
     fwd_out, bwd_out,
-    saved, arrived, returned, win, wout, packed, land, pre_f, pre_b, hidden, pre_grad,
+    saved, arrived, returned, win, wout, packing, placing, packed, land, pre_f, pre_b, hidden, pre_grad,
     own, cross, sib, pair_out, pair_in, total, back, result,
     send_a, recv_a, send_b, recv_b, send_c, recv_c, send_d, recv_d,
     send_s, recv_s, send_p, recv_p, send_r, recv_r, send_m, recv_m, load, store,
@@ -87,19 +90,16 @@
     peers = targets[1:] + sources[4:6] + [sibling, partner, after, before]
     for peer in peers:
         pl.semaphore_signal(barrier, inc=1, device_id=peer, device_id_type=MESH)
-    pl.semaphore_wait(barrier, len(peers))
 
     def remote(src, dst, send, recv, to):
         return pltpu.make_async_remote_copy(
             src_ref=src, dst_ref=dst, send_sem=send, recv_sem=recv, device_id=to, device_id_type=MESH
         )
 
-    moves = [
-        remote(fwd_in, arrived, send_m.at[0], recv_m.at[0], after),
-        remote(bwd_grad, returned, send_m.at[1], recv_m.at[1], before),
-    ]
-    for copy in moves:
-        copy.start()
+    def move(way, k):
+        columns = pl.ds(k * CHUNK, CHUNK)
+        src, dst, to = ((fwd_in, arrived, after), (bwd_grad, returned, before))[way]
+        return remote(src.at[:, columns], dst.at[:, columns], send_m.at[way, k], recv_m.at[way, k], to)
 
     def unit_experts(shape, dim):
         unit = lax.div(iota(shape, dim), ROWS)
@@ -108,34 +108,49 @@
             named = jnp.where(unit == u, experts[u], named)
         return named
 
-    def pack(flow, values, route):
+    def make_masks(way):
         square = (TOK, TOK)
-        by_row = jnp.broadcast_to(route[...], square).astype(F32)
-        by_lane = by_row.T
-        earlier = iota(square, 0) < iota(square, 1)
-        slot = jnp.sum(jnp.where((by_row == by_lane) & earlier, 1.0, 0.0), axis=0, keepdims=True)
+        route = (fwd_route, bwd_route)[way]
+        by_lane = jnp.broadcast_to(route[...], square).astype(F32)
+        by_row = by_lane.T
+        same = by_row == by_lane
+        lane, sublane = iota(square, 1), iota(square, 0)
+
+        slot = jnp.sum(jnp.where(same & (sublane < lane), 1.0, 0.0), axis=0, keepdims=True)
         named = unit_experts(square, 0).astype(F32) == by_lane
-        row = lax.rem(iota(square, 0), ROWS)
-        main = one_hot(named & (row.astype(F32) == slot))
+        row = lax.rem(sublane, ROWS)
+        packing[way, FOLD] = one_hot(named & (row.astype(F32) == slot))
         late = named & ((ROWS + lax.rem(row, 4)).astype(F32) == slot)
-
-        def put(k, rows):
-            packed[flow, k] = rows.astype(BF16)
-            land[flow, k, 0:ROWS] = packed[flow, k, 0:ROWS]
-            for u in range(1, UNITS):
-                block = pl.ds(u * ROWS, ROWS)
-                remote(
-                    packed.at[flow, k, block], land.at[flow, k, block],
-                    send_a.at[flow, k], recv_a.at[flow, k], targets[u],
-                ).start()
-
         for k in range(CHUNKS):
-            put(k, dot(main, values[:, k * CHUNK : (k + 1) * CHUNK]))
-        rows = jnp.zeros((ENTRY, CHUNK), F32)
+            packing[way, k] = one_hot(late & (lax.div(row, 4) == k))
+
+        slot = jnp.sum(jnp.where(same & (lane < sublane), 1.0, 0.0), axis=1, keepdims=True)
+        named = unit_experts(square, 1).astype(F32) == by_row
+        column = lax.rem(lane, ROWS)
+        placing[way, FOLD] = one_hot(named & (column.astype(F32) == slot))
+        late = named & ((ROWS + lax.rem(column, 4)).astype(F32) == slot)
         for k in range(CHUNKS):
-            mine = one_hot(late & (lax.div(row, 4) == k))
-            rows = rows + dot(mine, values[:, k * CHUNK : (k + 1) * CHUNK])
-        put(FOLD, rows)
+            placing[way, k] = one_hot(late & (lax.div(column, 4) == k))
+
+    def pack(flow, k):
+        values = (saved, arrived, returned)[flow]
+        way = FORWARD if flow == ARRIVED else BACKWARD
+        if k < CHUNKS:
+            rows = dot(packing[way, FOLD], values[:, k * CHUNK : (k + 1) * CHUNK])
+        else:
+            rows = jnp.zeros((ENTRY, CHUNK), F32)
+            for c in range(CHUNKS):
+                rows = rows + dot(packing[way, c], values[:, c * CHUNK : (c + 1) * CHUNK])
+        packed[flow, k] = rows.astype(BF16)
+        land[flow, k, 0:ROWS] = packed[flow, k, 0:ROWS]
+
+    def send(flow, k):
+        for u in range(1, UNITS):
+            block = pl.ds(u * ROWS, ROWS)
+            remote(
+                packed.at[flow, k, block], land.at[flow, k, block],
+                send_a.at[flow, k], recv_a.at[flow, k], targets[u],
+            ).start()
 
     def direct(flow, k):
         block = pl.ds(ROWS, ENTRY - ROWS)
@@ -171,11 +186,6 @@
         to_partner(flow, k).wait_recv()
         on_to_sibling(flow, k).start()
 
-    def ready(flow):
-        for k in range(CHUNKS + 1):
-            to_sibling(flow, k).wait_recv()
-            on_to_sibling(flow, k).wait_recv()
-
     def unfold(flow, k):
         shape = (LEFT, ALL_ROWS)
         row = iota(shape, 0)
@@ -188,14 +198,24 @@
         taken = lax.div(column, 4) * ROWS + k * 4 + lax.rem(column, 4)
         return dot(one_hot(iota(shape, 0) == taken), rows)
 
-    def activate_in(flow, out):
-        out[...] = jnp.zeros_like(out)
-
-        @pl.loop(0, CHUNKS)
-        def _(k):
-            weight = win[k]
-            out[0:ALL_ROWS] += dot(land[flow, k], weight)
-            out[ALL_ROWS:] += dot(unfold(flow, k), weight)
+    def digest(flow, k):
+        to_sibling(flow, k).wait_recv()
+        on_to_sibling(flow, k).wait_recv()
+        out = pre_b if flow == SAVED else pre_f
+        columns = slice(0, HID if flow == RETURNED else 2 * HID)
+
+        def times(rows, c):
+            return dot_t(rows, wout[c]) if flow == RETURNED else dot(rows, win[c])
+
+        if k == 0:
+            out[:ALL_ROWS, columns] = times(land[flow, k], k)
+        elif k < CHUNKS:
+            out[:ALL_ROWS, columns] += times(land[flow, k], k)
+        else:
+            rows = times(unfold(flow, 0), 0)
+            for c in range(1, CHUNKS):
+                rows = rows + times(unfold(flow, c), c)
+            out[ALL_ROWS:, columns] = rows
 
     def make_hidden():
         @pl.loop(0, (ALL_ROWS + LEFT) // LEFT)
@@ -205,14 +225,6 @@
             hidden[rows] = (gate_act * jax.nn.sigmoid(gate_act) * pre_f[rows, HID:]).astype(BF16)
 
     def make_pre_grad():
-        pre_f[...] = jnp.zeros_like(pre_f)
-
-        @pl.loop(0, CHUNKS)
-        def _(k):
-            weight = wout[k]
-            pre_f[0:ALL_ROWS, :HID] += dot_t(land[RETURNED, k], weight)
-            pre_f[ALL_ROWS:, :HID] += dot_t(unfold(RETURNED, k), weight)
-
         @pl.loop(0, (ALL_ROWS + LEFT) // LEFT)
         def _(n):
             rows = pl.ds(pl.multiple_of(n * LEFT, LEFT), LEFT)
@@ -285,81 +297,96 @@
         out = fwd_out if way == FORWARD else bwd_out
         return pltpu.make_async_copy(result.at[way, :, columns], out.at[:, columns], store.at[way, k])
 
+    def place_rows(way, k):
+        gate, base = ((fwd_gate, arrived), (bwd_gate, returned))[way]
+        weight = jnp.broadcast_to(gate[...], (TOK, TOK)).T[:, :1]
+        mixture = dot(placing[way, FOLD], back[way, k]) + dot(placing[way, k], back[way, FOLD])
+        at_columns = slice(k * CHUNK, (k + 1) * CHUNK)
+        rows = base[:, at_columns].astype(F32) + weight * mixture
+        result[way, :, at_columns] = rows.astype(BF16)
+        written(way, k).start()
+
     def finish(way, k):
         homeward(way, k).wait_recv()
-        if k == FOLD:
-            return
-        route, gate, base = (
-            (fwd_route, fwd_gate, arrived) if way == FORWARD else (bwd_route, bwd_gate, returned)
-        )
-        square = (TOK, TOK)
-        by_row = jnp.broadcast_to(route[...], square).astype(F32)
-        by_lane = by_row.T
-        earlier = iota(square, 1) < iota(square, 0)
-        slot = jnp.sum(jnp.where((by_row == by_lane) & earlier, 1.0, 0.0), axis=1, keepdims=True)
-        named = unit_experts(square, 1).astype(F32) == by_row
-        column = lax.rem(iota(square, 1), ROWS)
-        main = one_hot(named & (column.astype(F32) == slot))
-        late = named & ((ROWS + lax.rem(column, 4)).astype(F32) == slot)
-        mine = one_hot(late & (lax.div(column, 4) == k))
-        mixture = dot(main, back[way, k]) + dot(mine, back[way, FOLD])
-        at_columns = slice(k * CHUNK, (k + 1) * CHUNK)
-        result[way, :, at_columns] = (
-            base[:, at_columns].astype(F32) + gate[...] * mixture
-        ).astype(BF16)
-        written(way, k).start()
-
+        if k:
+            place_rows(way, 0 if k == FOLD else k)
+
+    make_masks(BACKWARD)
     loads[0].wait()
-    pack(SAVED, saved, bwd_route)
-    for k in range(CHUNKS + 1):
-        enter(SAVED, k)
-        if k:
-            pass_on(SAVED, k - 1)
-        if k == 3:
-            moves[0].wait_recv()
-            pack(ARRIVED, arrived, fwd_route)
-    pass_on(SAVED, FOLD)
-    for k in range(CHUNKS + 1):
-        enter(ARRIVED, k)
-        if k:
-            pass_on(ARRIVED, k - 1)
-        else:
-            for copy in loads[1:]:
-                copy.wait()
-            ready(SAVED)
-            activate_in(SAVED, pre_b)
-        if k == 3:
-            moves[1].wait_recv()
-            pack(RETURNED, returned, bwd_route)
-    pass_on(ARRIVED, FOLD)
-    for k in range(CHUNKS + 1):
-        enter(RETURNED, k)
-        if k:
-            pass_on(RETURNED, k - 1)
-        else:
-            ready(ARRIVED)
-            activate_in(ARRIVED, pre_f)
-            make_hidden()
-        work(FORWARD, ORDER[k])
-    pass_on(RETURNED, FOLD)
+    pack(SAVED, 0)
+    pl.semaphore_wait(barrier, len(peers))
+    send(SAVED, 0)
+    for k in range(1, CHUNKS + 1):
+        pack(SAVED, k)
+        if k < AHEAD:
+            send(SAVED, k)
+    make_masks(FORWARD)
+    for copy in loads[1:]:
+        copy.wait()
+
+    steps = []
+
+    def step(function, *arguments):
+        steps.append((function, arguments))
+
+    def take(flow, k):
+        if flow != SAVED:
+            if k < CHUNKS:
+                move(FORWARD if flow == ARRIVED else BACKWARD, k).wait_recv()
+            pack(flow, k)
+        send(flow, k)
+
+    def move_next(n):
+        for way in (FORWARD, BACKWARD):
+            if 0 <= n - MOVE_AT[way] < CHUNKS:
+                move(way, n - MOVE_AT[way]).start()
+
+    parts = CHUNKS + 1
+    for n in range(3 * parts):
+        flow, k = n // parts, n % parts
+        step(enter, flow, k)
+        step(move_next, n)
+        if n + AHEAD < 3 * parts:
+            step(take, (n + AHEAD) // parts, (n + AHEAD) % parts)
+        if n:
+            step(pass_on, (n - 1) // parts, (n - 1) % parts)
+        if n >= 2:
+            step(digest, (n - 2) // parts, (n - 2) % parts)
+        if flow == RETURNED:
+            if k == 1:
+                step(make_hidden)
+            if k >= 1:
+                step(work, FORWARD, ORDER[k - 1])
+            if k >= 2:
+                step(add_sibling, FORWARD, ORDER[k - 2])
+    step(pass_on, RETURNED, FOLD)
+    step(work, FORWARD, ORDER[4])
+    step(add_sibling, FORWARD, ORDER[3])
+    step(leave, FORWARD, ORDER[0])
+    step(add_sibling, FORWARD, ORDER[4])
+    step(digest, RETURNED, 3)
+    step(leave, FORWARD, ORDER[1])
+    step(digest, RETURNED, FOLD)
+    step(make_pre_grad)
+    for j, k in enumerate(ORDER):
+        if j >= 2:
+            step(leave, FORWARD, k)
+        step(work, BACKWARD, k)
+        if j and j <= LAG:
+            step(add_sibling, BACKWARD, ORDER[j - 1])
+    for j, k in enumerate(ORDER):
+        step(leave, BACKWARD, k)
+        if j + LAG < parts:
+            step(add_sibling, BACKWARD, ORDER[j + LAG])
+        step(finish, FORWARD, k)
     for k in ORDER:
-        add_sibling(FORWARD, k)
-    ready(RETURNED)
-    make_pre_grad()
-    for j, k in enumerate(ORDER):
-        leave(FORWARD, k)
-        work(BACKWARD, k)
-        if j:
-            add_sibling(BACKWARD, ORDER[j - 1])
-    add_sibling(BACKWARD, ORDER[-1])
-    for k in ORDER:
-        leave(BACKWARD, k)
-        finish(FORWARD, k)
-    for k in ORDER:
-        finish(BACKWARD, k)
-
-    for copy in moves:
-        copy.wait_send()
+        step(finish, BACKWARD, k)
+    for function, arguments in steps:
+        function(*arguments)
+
+    for way in (FORWARD, BACKWARD):
+        for k in range(CHUNKS):
+            move(way, k).wait_send()
     for flow in range(3):
         for k in range(CHUNKS + 1):
             direct(flow, k).wait_send()
@@ -373,6 +400,22 @@
     for way in (FORWARD, BACKWARD):
         for k in range(CHUNKS):
             written(way, k).wait()
+
+
+def copy_kernel(fwd_in, bwd_in, fwd_out, bwd_out):
+    fwd_out[0] = fwd_in[...]
+    bwd_out[0] = bwd_in[...]
+
+
+def keep(fwd_out, bwd_out):
+    rows = TOK // 4
+    return pl.pallas_call(
+        copy_kernel,
+        grid=(4,),
+        out_shape=[jax.ShapeDtypeStruct((1, TOK, D), BF16)] * 2,
+        in_specs=[pl.BlockSpec((rows, D), lambda n: (n, 0))] * 2,
+        out_specs=[pl.BlockSpec((1, rows, D), lambda n: (0, n, 0))] * 2,
+    )(fwd_out, bwd_out)
 
 
 def local(fwd_in, fwd_route, fwd_gate, bwd_saved, bwd_route, bwd_gate, bwd_grad, w_in, w_out):
@@ -392,6 +435,8 @@
             pltpu.VMEM(tokens, BF16),
             pltpu.VMEM((CHUNKS, CHUNK, 2 * HID), BF16),
             pltpu.VMEM((CHUNKS, HID, CHUNK), BF16),
+            pltpu.VMEM((2, parts, TOK, TOK), BF16),
+            pltpu.VMEM((2, parts, TOK, TOK), BF16),
             pltpu.VMEM((3, parts, ENTRY, CHUNK), BF16),
             pltpu.VMEM((3, parts, ALL_ROWS, CHUNK), BF16),
             pltpu.VMEM((ALL_ROWS + LEFT, 2 * HID), F32),
@@ -409,7 +454,7 @@
         ]
         + [dma((3, parts))] * 8
         + [dma((2, parts))] * 6
-        + [dma((2,))] * 2
+        + [dma((2, CHUNKS))] * 2
         + [dma((9,)), dma((2, CHUNKS))],
         compiler_params=pltpu.CompilerParams(
             collective_id=0, has_side_effects=True, vmem_limit_bytes=60 * 2**20
@@ -418,10 +463,11 @@
             flops=14 * 10**9, bytes_accessed=14 * 10**6, transcendentals=500_000
         ),
     )(
-        fwd_in[0], fwd_route[0], fwd_gate[0], bwd_saved[0], bwd_route[0], bwd_gate[0], bwd_grad[0],
+        fwd_in[0], fwd_route.reshape(1, TOK), fwd_gate.reshape(1, TOK),
+        bwd_saved[0], bwd_route.reshape(1, TOK), bwd_gate.reshape(1, TOK), bwd_grad[0],
         w_in[0, 0], w_out[0, 0],
     )
-    return fwd_out[None], bwd_out[None]
+    return keep(fwd_out, bwd_out)
 
 
 def solution(mesh):

time: 242 us -> 216 us (0.89)
  Pallas kernels: 231 us -> 215 us
  local copies, waits for them, and re-layouts: 9.87 us -> 0 us
    pallas_call x1, Pallas kernels: 231 us -> 211 us  [local(): pl.pallas_call(kernel, out_shape=[jax.ShapeDtypeStruct(tokens, BF16)] * 2...]
    squeeze x4 -> x0, local copies, waits for them, and re-layouts: 5.55 us -> none  [the longest x1 1.39 us: local(): fwd_route[0]]
    unnamed x2 -> x0, local copies, waits for them, and re-layouts: 4.32 us -> none
    pallas_call x0 -> x1, Pallas kernels: none -> 3.74 us  [keep(): pl.pallas_call(copy_kernel, grid=(4,), out_shape=[jax.ShapeDtypeStruct((1...]
where the time goes in v2:
time: 216 us; the launch traced here: 215 us
  Pallas kernels  215 us (100%)
    pallas_call x1, Pallas kernels, local(): pl.pallas_call(kernel, out_shape=[jax.ShapeDtypeStruct(tokens, BF16)] * 2...  211 us

profile of v2, /device:TPU:8, one launch (start us, length us, event | category | flops | bytes accessed | tf_op | source)
XLA Modules:
  0.0 215.4 jit_solution(2530206925963435459)
XLA Ops:
  0.6 211.1 %shard_map.104 = (bf16[128,3584]{1,0:T(8,128)(2,1)}, bf16[128,3584]{1,0:T(8,128)(2,1)}) custom-call(bf16[128,3584]{1,0:T(8,128)(2,1)} %bitcast.11, s32[1,128]{1,0:T(1,128)} %bitcast.14, f32[1,128]{1,0:T(1,128)} %bitcast.15, bf16[128,3584]{1,0:T(8,128)(2,1)} %bitcast.12, s32[1,128]{1,0:T(1,128)} %bitcast.16, f32[1,128]{1,0:T(1,128)} %bitcast.17, ...), custom_call_target="tpu_custom_call" | custom-call | flops 14000000000 | bytes 14000000 | tf_op jit(solution)/shard_map/pallas_call | solution.py:427
  211.7 3.7 %shard_map.105 = (bf16[1,128,3584]{2,1,0:T(8,128)(2,1)}, bf16[1,128,3584]{2,1,0:T(8,128)(2,1)}) custom-call(bf16[128,3584]{1,0:T(8,128)(2,1)} %get-tuple-element.4.fwd_in, bf16[128,3584]{1,0:T(8,128)(2,1)} %get-tuple-element.5.bwd_in), custom_call_target="tpu_custom_call" | custom-call | tf_op jit(solution)/shard_map/pallas_call | solution.py:412

commit v3 on v2

--- a/solution.py
+++ b/solution.py
@@ -6,6 +6,7 @@
 from jax.sharding import PartitionSpec as P
 
 MESH = pl.DeviceIdType.MESH
+SCHEDULE = ((), ((0, 0),), ((0, 1),), ((0, 2),), ((0, 3), (1, 0), (1, 1)))
 TOK = 128
 D = 3584
 HID = 384
@@ -14,14 +15,15 @@
 CHUNKS = 4
 FOLD = 4
 UNITS = 8
+PIECES = 4
 ENTRY = UNITS * ROWS
 ALL_ROWS = 4 * ENTRY
 LEFT = 128
 OFFSETS = (0, -1, 2, -3)
 ORDER = (0, 4, 1, 2, 3)
-MOVE_AT = (0, 4)
+MOVE_AT = (0, 3)
 LAG = 4
-AHEAD = 5
+AHEAD = 4
 SAVED, ARRIVED, RETURNED = 0, 1, 2
 FORWARD, BACKWARD = 0, 1
 F32 = jnp.float32
@@ -355,18 +357,16 @@
         if flow == RETURNED:
             if k == 1:
                 step(make_hidden)
-            if k >= 1:
-                step(work, FORWARD, ORDER[k - 1])
-            if k >= 2:
-                step(add_sibling, FORWARD, ORDER[k - 2])
+            for function, number in SCHEDULE[k]:
+                step((work, add_sibling, leave)[function], FORWARD, ORDER[number])
     step(pass_on, RETURNED, FOLD)
     step(work, FORWARD, ORDER[4])
-    step(add_sibling, FORWARD, ORDER[3])
+    for number in (2, 3, 4):
+        step(add_sibling, FORWARD, ORDER[number])
+    step(digest, RETURNED, 3)
     step(leave, FORWARD, ORDER[0])
-    step(add_sibling, FORWARD, ORDER[4])
-    step(digest, RETURNED, 3)
+    step(digest, RETURNED, FOLD)
     step(leave, FORWARD, ORDER[1])
-    step(digest, RETURNED, FOLD)
     step(make_pre_grad)
     for j, k in enumerate(ORDER):
         if j >= 2:
@@ -402,19 +402,31 @@
             written(way, k).wait()
 
 
-def copy_kernel(fwd_in, bwd_in, fwd_out, bwd_out):
-    fwd_out[0] = fwd_in[...]
-    bwd_out[0] = bwd_in[...]
+def copy_kernel(fwd_in, bwd_in, fwd_out, bwd_out, held, read, wrote):
+    reads, writes = [], []
+    for way, (src, dst) in enumerate(((fwd_in, fwd_out), (bwd_in, bwd_out))):
+        for n in range(PIECES):
+            rows = pl.ds(n * (TOK // PIECES), TOK // PIECES)
+            reads.append(pltpu.make_async_copy(src.at[rows], held.at[way, rows], read.at[way, n]))
+            writes.append(pltpu.make_async_copy(held.at[way, rows], dst.at[0, rows], wrote.at[way, n]))
+    for copy in reads:
+        copy.start()
+    for arrived, leaving in zip(reads, writes):
+        arrived.wait()
+        leaving.start()
+    for copy in writes:
+        copy.wait()
 
 
 def keep(fwd_out, bwd_out):
-    rows = TOK // 4
+    any_place = pl.BlockSpec(memory_space=pl.ANY)
+    dma = pltpu.SemaphoreType.DMA
     return pl.pallas_call(
         copy_kernel,
-        grid=(4,),
         out_shape=[jax.ShapeDtypeStruct((1, TOK, D), BF16)] * 2,
-        in_specs=[pl.BlockSpec((rows, D), lambda n: (n, 0))] * 2,
-        out_specs=[pl.BlockSpec((1, rows, D), lambda n: (0, n, 0))] * 2,
+        in_specs=[any_place] * 2,
+        out_specs=[any_place] * 2,
+        scratch_shapes=[pltpu.VMEM((2, TOK, D), BF16), dma((2, PIECES)), dma((2, PIECES))],
     )(fwd_out, bwd_out)
 
 

time: 216 us -> 211 us (0.977)
  Pallas kernels: 215 us -> 209 us
    pallas_call x1, Pallas kernels: 211 us -> 206 us  [local(): pl.pallas_call(kernel, out_shape=[jax.ShapeDtypeStruct(tokens, BF16)] * 2...]
where the time goes in v3:
time: 211 us; the launch traced here: 209 us
  Pallas kernels  209 us (99%)
    pallas_call x1, Pallas kernels, local(): pl.pallas_call(kernel, out_shape=[jax.ShapeDtypeStruct(tokens, BF16)] * 2...  206 us

profile of v3, /device:TPU:8, one launch (start us, length us, event | category | flops | bytes accessed | tf_op | source)
XLA Modules:
  0.0 209.4 jit_solution(16624688768979299705)
XLA Ops:
  0.6 206.1 %shard_map.104 = (bf16[128,3584]{1,0:T(8,128)(2,1)}, bf16[128,3584]{1,0:T(8,128)(2,1)}) custom-call(bf16[128,3584]{1,0:T(8,128)(2,1)} %bitcast.11, s32[1,128]{1,0:T(1,128)} %bitcast.14, f32[1,128]{1,0:T(1,128)} %bitcast.15, bf16[128,3584]{1,0:T(8,128)(2,1)} %bitcast.12, s32[1,128]{1,0:T(1,128)} %bitcast.16, f32[1,128]{1,0:T(1,128)} %bitcast.17, ...), custom_call_target="tpu_custom_call" | custom-call | flops 14000000000 | bytes 14000000 | tf_op jit(solution)/shard_map/pallas_call | solution.py:439
  206.8 2.4 %shard_map.105 = (bf16[1,128,3584]{2,1,0:T(8,128)(2,1)}, bf16[1,128,3584]{2,1,0:T(8,128)(2,1)}) custom-call(bf16[128,3584]{1,0:T(8,128)(2,1)} %get-tuple-element.4.fwd_in, bf16[128,3584]{1,0:T(8,128)(2,1)} %get-tuple-element.5.bwd_in), custom_call_target="tpu_custom_call" | custom-call | tf_op jit(solution)/shard_map/pallas_call | solution.py:424
